TPU v7x, 128 devices: a whole 4x4x4 slice. The times are simulated.
128 devices in a mesh: front: 32 (over z, y, x_lo), row: 2 (over core), col: 2 (over x_hi).
Axes of the slice: x: 4 (x_hi: 2, x_lo: 2; x = x_hi * 2 + x_lo), y: 4, z: 4, core: 2. Of those that a mesh axis runs over, the one named last changes fastest.
Arguments:
- front: bfloat16 [32, 4096, 4096], P('front', 'row', 'col'), may hold values from -6 to 30
- inverses: bfloat16 [32, 2, 256, 256], P('front'), may hold values from -0.2 to 0.2
- routes: int32 [32, 16, 16], P('front', 'row', 'col'), may hold values from -1 to 31, as said below
- positions: int32 [32, 16, 16], P('front', 'row', 'col'), may hold values from 0 to 63
- parent: bfloat16 [32, 4096, 4096], P('front', 'row', 'col'), may hold values from -6 to 6
Outputs:
- factor: bfloat16 [32, 4096, 512], P('front', 'row', 'col')
- parent_out: bfloat16 [32, 4096, 4096], P('front', 'row', 'col')
Inputs may be any that keep to these rules, and one draw needn't show every extreme that they name: `routes`: -1 exactly on blocks whose block row or block column is under 2; at most 2 blocks held by one device name one group, and in every draw some group is named by exactly 2 blocks of every device of some grid position. `positions`: a block of the receiving device's share of the parent front, counted row by row.
All inputs are finite; a program needn't handle non-finite values.
Results may differ from a plain program's by a relative error of at most 0.0055.
Values may be sent and summed in bfloat16 or wider, within the bound.
A program may use at most 192 MiB of HBM per device.

v0:
```python
import jax
import jax.numpy as jnp
from jax import lax
from jax.sharding import PartitionSpec as P


def from_root(value, axis, source):
    kept = jnp.where(lax.axis_index(axis) == source, value, 0).astype(value.dtype)
    return lax.psum(kept, axis)


def body(front, inverses, routes, positions, parent):
    matrix = front[0].astype(jnp.float32)
    row_len = matrix.shape[0]
    col_len = matrix.shape[1]
    blk_size = inverses.shape[-1]
    panel_count = inverses.shape[1]
    row_index = lax.axis_index("row")
    col_index = lax.axis_index("col")
    global_rows = row_index * row_len + jnp.arange(row_len)

    def pieces_of(work, panel):
        lower = panel * blk_size
        col_start = lower - lower // col_len * col_len
        row_start = lower - lower // row_len * row_len
        return (
            work[:, col_start : col_start + blk_size].astype(jnp.bfloat16),
            work[row_start : row_start + blk_size, :].astype(jnp.bfloat16),
        )

    pieces = pieces_of(matrix, 0)
    factors = []
    for panel in range(panel_count):
        lower = panel * blk_size
        column = from_root(pieces[0], "col", lower // col_len)
        block_row = from_root(pieces[1], "row", lower // row_len)
        product = jnp.dot(column, inverses[0, panel], preferred_element_type=jnp.float32)
        panel_factor = jnp.where(global_rows[:, None] >= lower, product, 0.0).astype(jnp.bfloat16)
        factors.append(panel_factor)
        if panel + 1 < panel_count:
            matrix = matrix - jnp.dot(panel_factor, block_row, preferred_element_type=jnp.float32)
            pieces = pieces_of(matrix, panel + 1)
        else:
            matrix = matrix - jnp.dot(panel_factor, block_row, preferred_element_type=jnp.float32)
    joined = jnp.concatenate(factors, axis=1)
    out_width = joined.shape[1] // lax.axis_size("col")
    factor_out = lax.dynamic_slice_in_dim(joined, col_index * out_width, out_width, 1)[None]
    row_blocks = row_len // blk_size
    col_blocks = col_len // blk_size
    tile_count = row_blocks * col_blocks
    tile_area = blk_size * blk_size
    tiles = (
        matrix.reshape(row_blocks, blk_size, col_blocks, blk_size)
        .transpose(0, 2, 1, 3)
        .reshape(tile_count, tile_area)
    )
    route = routes[0].reshape(tile_count)
    place = positions[0].reshape(tile_count)
    group_count = lax.axis_size("front")
    capacity = (tile_count + group_count - 1) // group_count
    slot_count = group_count * capacity
    valid = route >= 0
    order_ids = jnp.arange(tile_count)
    earlier = jnp.sum(
        ((route[:, None] == route[None, :]) & (order_ids[None, :] < order_ids[:, None])).astype(
            jnp.int32
        ),
        axis=1,
    )
    slot = route * capacity + earlier
    send_table = ((slot[:, None] == jnp.arange(slot_count)[None, :]) & valid[:, None]).astype(
        jnp.float32
    )
    outgoing = jnp.dot(
        send_table.T, tiles, precision=lax.Precision.HIGHEST, preferred_element_type=jnp.float32
    ).reshape(group_count, capacity, tile_area)
    out_place = jnp.dot(
        send_table.T,
        (place + 1).astype(jnp.float32),
        precision=lax.Precision.HIGHEST,
        preferred_element_type=jnp.float32,
    ).reshape(group_count, capacity)
    incoming, in_place = (
        lax.all_to_all(outgoing, "front", split_axis=0, concat_axis=0, tiled=True),
        lax.all_to_all(out_place, "front", split_axis=0, concat_axis=0, tiled=True),
    )
    recv_table = (
        in_place.reshape(slot_count)[:, None] - 1.0
        == jnp.arange(tile_count, dtype=jnp.float32)[None, :]
    ).astype(jnp.float32)
    added = jnp.dot(
        recv_table.T,
        incoming.reshape(slot_count, tile_area),
        precision=lax.Precision.HIGHEST,
        preferred_element_type=jnp.float32,
    )
    parent_tiles = (
        parent[0]
        .astype(jnp.float32)
        .reshape(row_blocks, blk_size, col_blocks, blk_size)
        .transpose(0, 2, 1, 3)
    )
    summed = parent_tiles + added.reshape(row_blocks, col_blocks, blk_size, blk_size)
    parent_out = summed.transpose(0, 2, 1, 3).reshape(row_len, col_len).astype(jnp.bfloat16)[None]
    return (factor_out, parent_out)


def solution(mesh):
    return jax.shard_map(
        body,
        mesh=mesh,
        in_specs=(
            P("front", "row", "col"),
            P("front", None, None, None),
            P("front", "row", "col"),
            P("front", "row", "col"),
            P("front", "row", "col"),
        ),
        out_specs=(P("front", "row", "col"), P("front", "row", "col")),
        check_vma=False,
    )
```

profile of v0, /device:TPU:26, one launch (start us, length us, event | category | flops | bytes accessed | tf_op | source)
XLA Modules:
  0.0 611.1 jit_solution(15935142128633197400)
XLA Ops:
  7.2 0.0 all-reduce.5.cloned.1.call-start
  7.2 2.3 slice_select_fusion.2
  9.5 0.0 all-reduce.5.cloned.1.call-update
  9.5 0.0 all-reduce.7.cloned.1.call-start
  9.6 2.3 select_bitcast_fusion
  11.8 0.0 all-reduce.7.cloned.1.call-update
  11.9 0.0 all-reduce.9.cloned.1.call-start
  11.9 48.4 %all-reduce.5.cloned.1.call-done = bf16[2048,256]{1,0:T(8,128)(2,1)} async-done(((bf16[2048,256]{1,0:T(8,128)(2,1)}), bf16[2048,256]{1,0:T(8,128)(2,1)}) %all-reduce.5.cloned.1.call-update) | async-done | bytes 1048592 | tf_op jit(solution)/shard_map/psum | solution.py:9
  60.4 1.7 fusion.5
  62.1 0.0 copy-start.1
  62.1 0.0 copy-start.2
  62.1 0.0 copy-start.3
  62.1 27.0 %all-reduce.7.cloned.1.call-done = bf16[256,2048]{1,0:T(8,128)(2,1)} async-done(((bf16[256,2048]{1,0:T(8,128)(2,1)}), bf16[256,2048]{1,0:T(8,128)(2,1)}) %all-reduce.7.cloned.1.call-update) | async-done | bytes 1048592 | tf_op jit(solution)/shard_map/psum | solution.py:9
  89.2 11.8 %fusion.4 = (bf16[2048,2048]{1,0:T(8,128)(2,1)S(1)}, f32[2048,2048]{1,0:T(8,128)}) fusion(bf16[1,2048,2048]{2,1,0:T(8,128)(2,1)} %param.5, bf16[2048,256]{0,1:T(8,128)(2,1)S(1)} %fusion.5, bf16[256,2048]{1,0:T(8,128)(2,1)} %all-reduce.7.cloned.1.call-done), kind=kOutput, calls=%fused_computation.7 | convolution fusion | flops 2160066560 | bytes 35651584 | tf_op jit(solution)/shard_map/dot_general | solution.py:41
  101.0 0.0 copy-start
  101.0 3.4 copy-done
  104.4 1.1 slice_select_fusion.1
  105.5 0.0 all-reduce.9.cloned.1.call-update
  105.5 0.0 all-reduce.11.cloned.1.call-start
  105.6 0.0 copy-done.1
  105.6 0.1 reshape_squeeze.4
  105.7 0.0 copy-done.2
  105.7 0.1 reshape.145
  105.8 0.2 convert_reduce_fusion
  106.0 2.3 slice_select_fusion
  108.3 0.0 all-reduce.11.cloned.1.call-update
  108.3 0.2 fusion.16
  108.5 0.8 copy.17
  109.3 8.4 %all-to-all-start = ((f32[32,1,2]{2,1,0:T(1,128)}), f32[32,1,2]{2,1,0:T(1,128)S(1)}, u32[]{:S(2)}, u32[]{:S(2)}) async-start(f32[32,1,2]{2,1,0:T(1,128)} %copy.17), calls=%async_computation | async-start | bytes 32768 | tf_op jit(solution)/shard_map/all_to_all | solution.py:85
  117.8 36.6 %all-reduce.9.cloned.1.call-done = bf16[2048,256]{1,0:T(8,128)(2,1)} async-done(((bf16[2048,256]{1,0:T(8,128)(2,1)}), bf16[2048,256]{1,0:T(8,128)(2,1)}) %all-reduce.9.cloned.1.call-update) | async-done | bytes 1048592 | tf_op jit(solution)/shard_map/psum | solution.py:9
  154.3 0.0 copy-done.3
  154.3 1.7 fusion.6
  156.1 26.4 %all-reduce.11.cloned.1.call-done = bf16[256,2048]{1,0:T(8,128)(2,1)} async-done(((bf16[256,2048]{1,0:T(8,128)(2,1)}), bf16[256,2048]{1,0:T(8,128)(2,1)}) %all-reduce.11.cloned.1.call-update) | async-done | bytes 1048592 | tf_op jit(solution)/shard_map/psum | solution.py:9
  182.4 16.6 %fusion.3 = f32[2048,2048]{1,0:T(8,128)} fusion(f32[2048,2048]{1,0:T(8,128)} %get-tuple-element.3, bf16[2048,256]{0,1:T(8,128)(2,1)S(1)} %fusion.6, bf16[256,2048]{1,0:T(8,128)(2,1)} %all-reduce.11.cloned.1.call-done, bf16[1,2048,2048]{2,1,0:T(8,128)(2,1)} %param.5), kind=kOutput, calls=%fused_computation.6 | convolution fusion | flops 2160066560 | bytes 44040192 | tf_op jit(solution)/shard_map/dot_general | solution.py:44
  199.0 15.7 %copy.24 = f32[256,8,8,256]{3,2,1,0:T(8,128)} copy(f32[256,8,8,256]{3,1,2,0:T(8,128)} %bitcast.67) | data formatting | bytes 33554432
  214.7 16.1 %fusion.15 = f32[32,2,65536]{2,0,1:T(8,128)} fusion(f32[64,65536,1]{1,0,2:T(8,128)} %bitcast.65, s32[32,2]{0,1:T(2,128)S(1)} %multiply_add_fusion.1, s32[64]{0:T(128)S(1)} %multiply_add_fusion.2, pred[64]{0:T(512)(128)(4,1)S(1)} %broadcast_compare_fusion), kind=kOutput, calls=%fused_computation.29 | convolution fusion | flops 3221233664 | bytes 33555008 | tf_op jit(solution)/shard_map/dot_general | solution.py:74
  230.8 28.5 %copy.18 = f32[32,2,65536]{2,1,0:T(2,128)} copy(f32[32,2,65536]{2,0,1:T(8,128)} %fusion.15) | data formatting | bytes 33554432 | tf_op jit(solution)/shard_map/dot_general | solution.py:74
  259.3 0.0 all-to-all-done
  259.3 8.5 %all-to-all-start.1 = ((f32[32,2,65536]{2,1,0:T(2,128)}), f32[32,2,65536]{2,1,0:T(2,128)}, u32[]{:S(2)}, u32[]{:S(2)}) async-start(f32[32,2,65536]{2,1,0:T(2,128)} %copy.18), calls=%async_computation.1 | async-start | bytes 33554432 | tf_op jit(solution)/shard_map/all_to_all | solution.py:84
  267.9 13.4 %copy.23 = f32[256,8,8,256]{3,2,1,0:T(8,128)} copy(bf16[256,8,8,256]{3,1,2,0:T(8,128)(2,1)} %bitcast.68) | data formatting | bytes 25165824
  281.3 0.1 sub.14
  281.4 0.9 fusion.7
  282.3 1.3 copy.16
  283.6 270.9 %all-to-all-done.1 = f32[32,2,65536]{2,1,0:T(2,128)} async-done(((f32[32,2,65536]{2,1,0:T(2,128)}), f32[32,2,65536]{2,1,0:T(2,128)}, u32[]{:S(2)}, u32[]{:S(2)}) %all-to-all-start.1) | async-done | bytes 16777248 | tf_op jit(solution)/shard_map/all_to_all | solution.py:84
  554.5 17.6 %reshape.143 = f32[64,65536]{1,0:T(8,128)} reshape(f32[32,2,65536]{2,1,0:T(2,128)} %all-to-all-done.1) | data formatting | bytes 33554432 | tf_op jit(solution)/shard_map/reshape | solution.py:93
  572.2 19.0 %fusion = bf16[8,256,8,256]{3,2,1,0:T(8,128)(2,1)} fusion(f32[8,256,8,256]{3,2,1,0:T(8,128)} %bitcast.66, f32[8,8]{1,0:T(8,128)S(1)} %multiply_add_fusion, f32[64]{0:T(128)S(1)} %sub.14, f32[8,256,8,256]{3,2,1,0:T(8,128)} %bitcast.64), kind=kOutput, calls=%fused_computation.1 | convolution fusion | flops 3229618176 | bytes 41943552 | tf_op jit(solution)/shard_map/dot_general | solution.py:91
  591.1 13.4 %convert_element_type.64 = bf16[1,2048,2048]{2,1,0:T(8,128)(2,1)} reshape(bf16[8,256,8,256]{3,2,1,0:T(8,128)(2,1)} %fusion) | data formatting | bytes 16777216 | tf_op jit(solution)/shard_map/convert_element_type | solution.py:104
  (8 shorter events, 0.1 us)
Async XLA Ops:
  7.2 53.2 %all-reduce.5.cloned.1.call-start = ((), (), s32[]{:S(2)}) async-start(), calls=%async_computation.2 | async-start | bytes 2097152 | tf_op jit(solution)/shard_map/psum | solution.py:9
  9.5 79.6 %all-reduce.7.cloned.1.call-start = ((), (), s32[]{:S(2)}) async-start(), calls=%async_computation.3 | async-start | bytes 2097152 | tf_op jit(solution)/shard_map/psum | solution.py:9
  11.9 142.5 %all-reduce.9.cloned.1.call-start = ((), (), s32[]{:S(2)}) async-start(), calls=%async_computation.4 | async-start | bytes 2097152 | tf_op jit(solution)/shard_map/psum | solution.py:9
  62.1 43.5 %copy-start.1 = (s32[1,8,8]{2,1,0:T(8,128)S(1)}, s32[1,8,8]{2,1,0:T(8,128)}, u32[]{:S(2)}) copy-start(s32[1,8,8]{2,1,0:T(8,128)} %param.7) | copy-start | bytes 772
  62.1 43.6 %copy-start.2 = (s32[1,8,8]{2,1,0:T(8,128)S(1)}, s32[1,8,8]{2,1,0:T(8,128)}, u32[]{:S(2)}) copy-start(s32[1,8,8]{2,1,0:T(8,128)} %param.8) | copy-start | bytes 772
  62.1 92.3 %copy-start.3 = (bf16[1,2,256,256]{3,2,1,0:T(8,128)(2,1)S(1)}, bf16[1,2,256,256]{3,2,1,0:T(8,128)(2,1)}, u32[]{:S(2)}) copy-start(bf16[1,2,256,256]{3,2,1,0:T(8,128)(2,1)} %param.6) | copy-start | bytes 786436
  101.0 3.4 copy-start
  105.5 76.9 %all-reduce.11.cloned.1.call-start = ((), (), s32[]{:S(2)}) async-start(), calls=%async_computation.5 | async-start | bytes 2097152 | tf_op jit(solution)/shard_map/psum | solution.py:9
  109.3 150.0 %all-to-all-start = ((f32[32,1,2]{2,1,0:T(1,128)}), f32[32,1,2]{2,1,0:T(1,128)S(1)}, u32[]{:S(2)}, u32[]{:S(2)}) async-start(f32[32,1,2]{2,1,0:T(1,128)} %copy.17), calls=%async_computation | async-start | bytes 32768 | tf_op jit(solution)/shard_map/all_to_all | solution.py:85
  259.3 295.2 %all-to-all-start.1 = ((f32[32,2,65536]{2,1,0:T(2,128)}), f32[32,2,65536]{2,1,0:T(2,128)}, u32[]{:S(2)}, u32[]{:S(2)}) async-start(f32[32,2,65536]{2,1,0:T(2,128)} %copy.18), calls=%async_computation.1 | async-start | bytes 33554432 | tf_op jit(solution)/shard_map/all_to_all | solution.py:84
Sparse Core Ops, SparseCore 0:
  11.0 49.2 all-reduce.4
  63.5 25.5 all-reduce.6
  105.7 48.6 all-reduce.8
  156.8 25.5 all-reduce.10
where the time goes:
time: 612 us; the launch traced here: 611 us
  waiting for transfers between devices  409 us (67%)
  local copies, waits for them, and re-layouts  94.4 us (15%)
  matrix products  67.1 us (11%)
  starting transfers between devices  17.1 us (3%)
  between operations  13.9 us (2%)
  other arithmetic  9.15 us (1%)
    all_to_all x1, waiting for transfers between devices, body(): lax.all_to_all(outgoing, 'front', split_axis=0, concat_axis=0, tiled=True)  271 us
    psum x4, waiting for transfers between devices, from_root(): return lax.psum(kept, axis)  138 us
    unnamed x10, local copies, waits for them, and re-layouts  32.5 us
    dot_general x1, local copies, waits for them, and re-layouts, body(): jnp.dot(send_table.T, tiles, precision=lax.Precision.HIGHEST, preferred_e...  28.5 us
    dot_general x2, matrix products, body(): jnp.dot(panel_factor, block_row, preferred_element_type=jnp.float32)  28.4 us
    dot_general x1, matrix products, body(): jnp.dot(recv_table.T, incoming.reshape(slot_count, tile_area), precision=...  19 us
    reshape x1, local copies, waits for them, and re-layouts, body(): incoming.reshape(slot_count, tile_area)  17.6 us
    dot_general x1, matrix products, body(): jnp.dot(send_table.T, tiles, precision=lax.Precision.HIGHEST, preferred_e...  16.1 us
  transfers between devices with their start and end apart: 6, of which 5 were waited for; matrix products, arithmetic and copies ran while one was open for 17% of the time, Pallas kernels for 0%

commit v1 on v0

v1 whole, which is shorter than its diff:
```python
import functools

import jax
import jax.numpy as jnp
from jax import lax
from jax.experimental import pallas as pl
from jax.experimental.pallas import tpu as pltpu
from jax.sharding import PartitionSpec as P

MESH = pl.DeviceIdType.MESH
NB = 256
SIDE = 8
TILES = SIDE * SIDE
GROUPS = 32
WIDTH = SIDE * NB
CHUNKS = (64, 64, 64, 64)
STARTS = tuple(sum(CHUNKS[:q]) for q in range(len(CHUNKS)))
NQ = len(CHUNKS)
F32 = jnp.float32
BF16 = jnp.bfloat16


def hops(d):
    return min(d[0], 4 - d[0]) + min(d[1], 4 - d[1]) + d[2]


OFFSETS = [(z, y, x) for z in range(4) for y in range(4) for x in range(2)]
ORDER = sorted(OFFSETS[1:], key=lambda d: -hops(d))


def dot(a, b):
    return jnp.dot(a, b, preferred_element_type=F32)


def kernel(front, inv, routes, places, parent, fac_out, out, *refs):
    refs = list(refs)

    def take(n):
        got = refs[:n]
        del refs[:n]
        return got

    c_bufs, a_bufs, p_bufs, f_bufs, s_bufs, r_bufs = (take(NQ) for _ in range(6))
    (b_buf, dt, l_buf, tiles, acc, pos_send, pos_recv, tab_v, tab_s, got_v, got_s) = take(11)
    (c_ss, c_rs, a_sem, p_sem, f_sem, o_sem, x_ss, x_rs, pos_ss, pos_rs) = take(10)
    (b_ss, b_rs, dt_ss, dt_rs, t_sem) = take(5)

    me = lax.axis_index("front")
    r = lax.axis_index("row")
    c = lax.axis_index("col")
    z, y, x = me // 8, (me // 2) % 4, me % 2
    sign = jnp.where(r == 0, 1, 3)

    def peer(d):
        return ((z + sign * d[0]) % 4) * 8 + ((y + sign * d[1]) % 4) * 2 + (x + d[2]) % 2

    def rows(q):
        return pl.ds(STARTS[q], CHUNKS[q])

    a_cps = [
        pltpu.make_async_copy(front.at[:, rows(q), :], a_bufs[q], a_sem.at[q]) for q in range(NQ)
    ]
    p_cps = [
        pltpu.make_async_copy(parent.at[:, rows(q), :], p_bufs[q], p_sem.at[q]) for q in range(NQ)
    ]
    c_loc = [
        pltpu.make_async_copy(front.at[:, rows(q), pl.ds(0, 2 * NB)], c_bufs[q], c_rs.at[q])
        for q in range(NQ)
    ]
    b_loc = pltpu.make_async_copy(front.at[pl.ds(0, 2)], b_buf, b_rs)

    @pl.when(r == 0)
    def _():
        b_loc.start()

    @pl.when(c == 0)
    def _():
        for cp in c_loc:
            cp.start()

    for cp in a_cps:
        cp.start()

    bar = pltpu.get_barrier_semaphore()

    def greet(k, _):
        pl.semaphore_signal(
            bar, 1, device_id=((me + k) % GROUPS, r, c), device_id_type=MESH
        )
        return 0

    lax.fori_loop(1, GROUPS, greet, 0)
    pl.semaphore_signal(bar, 1, device_id=(me, 1 - r, c), device_id_type=MESH)
    pl.semaphore_signal(bar, 1, device_id=(me, r, 1 - c), device_id_type=MESH)
    pl.semaphore_signal(bar, 1, device_id=(me, 1 - r, 1 - c), device_id_type=MESH)
    pl.semaphore_wait(bar, GROUPS + 2)

    def dt_copy(i, row):
        if i == 0:
            src = front.at[0, :, pl.ds(NB, NB)]
        else:
            src = front.at[1, :, pl.ds(0, NB)]
        return pltpu.make_async_remote_copy(
            src, dt.at[i], dt_ss.at[i, row], dt_rs.at[i], device_id=(me, row, 1), device_id_type=MESH
        )

    def c_copy(q, low):
        return pltpu.make_async_remote_copy(
            front.at[pl.ds(low, SIDE - low), rows(q), pl.ds(0, 2 * NB)],
            c_bufs[q].at[pl.ds(low, SIDE - low)],
            c_ss.at[q],
            c_rs.at[q],
            device_id=(me, r, 1),
            device_id_type=MESH,
        )

    b_copy = pltpu.make_async_remote_copy(
        front.at[pl.ds(0, 2)], b_buf, b_ss, b_rs, device_id=(me, 1, c), device_id_type=MESH
    )

    @pl.when((r == 0) & (c == 0))
    def _():
        for row in range(2):
            for i in range(2):
                dt_copy(i, row).start()

    @pl.when(r == 0)
    def _():
        b_copy.start()

    for row in range(2):

        @pl.when((r == row) & (c == 0))
        def _():
            for q in range(NQ):
                c_copy(q, 1 - row).start()

    for cp in p_cps:
        cp.start()

    @pl.when((r == 0) & (c == 1))
    def _():
        for q in range(NQ):
            c_bufs[q][0] = jnp.zeros((CHUNKS[q], 2 * NB), BF16)

    lane = lax.broadcasted_iota(jnp.int32, (TILES, 128), 1)
    sub = lax.broadcasted_iota(jnp.int32, (TILES, 128), 0)
    lane1 = lax.broadcasted_iota(jnp.int32, (1, 128), 1)

    def spread(t, carry):
        across, down, place = carry
        route = routes[t // SIDE, t % SIDE]
        across = jnp.where(lane1 == t, route, across)
        down = jnp.where(sub == t, route, down)
        place = jnp.where(lane1 == t, places[t // SIDE, t % SIDE], place)
        return across, down, place

    none1 = jnp.full((1, 128), -1, jnp.int32)
    across, down, place = lax.fori_loop(
        0, TILES, spread, (none1, jnp.full((TILES, 128), -1, jnp.int32), none1)
    )
    same = down == across
    before = jnp.sum(jnp.where(same & (sub < lane), 1, 0), axis=0, keepdims=True)
    slot8 = jnp.where((across >= 0) & (before < 2), across * 8 + before, -1)
    sub8 = lax.broadcasted_iota(jnp.int32, (GROUPS * 8, 128), 0)
    pos = jnp.max(jnp.where(slot8 == sub8, place, -1), axis=1, keepdims=True)
    pos_send[...] = jnp.broadcast_to(pos, (GROUPS * 8, 128))
    before = jnp.sum(jnp.where(same & (lane < sub), 1, 0), axis=1, keepdims=True)
    slot2 = jnp.where(down >= 0, down * 2 + before, -1)
    tab_v[...] = jnp.broadcast_to(
        jnp.max(jnp.where(slot2 == lane, sub, 0), axis=0, keepdims=True), (8, 128)
    )
    tab_cp = pltpu.make_async_copy(tab_v, tab_s, t_sem.at[0])
    tab_cp.start()
    pos_recv[pl.ds(0, 8), :] = pos_send[pl.ds(pl.multiple_of(me * 8, 8), 8), :]

    def pos_copy(d):
        k = OFFSETS.index(d)
        g = peer(d)
        return pltpu.make_async_remote_copy(
            pos_send.at[pl.ds(pl.multiple_of(g * 8, 8), 8)],
            pos_recv.at[pl.ds(8 * k, 8)],
            pos_ss.at[k],
            pos_rs.at[k],
            device_id=(g, r, c),
            device_id_type=MESH,
        )

    for d in ORDER:
        pos_copy(d).start()

    @pl.when(r == 0)
    def _():
        b_loc.wait()

    @pl.when(r == 1)
    def _():
        b_copy.wait_recv()

    @pl.when(c == 0)
    def _():
        dt[0] = b_buf[0, :, pl.ds(NB, NB)]
        dt[1] = b_buf[1, :, pl.ds(0, NB)]

    @pl.when(c == 1)
    def _():
        for i in range(2):
            dt_copy(i, 0).wait_recv()

    panel_d = dot(dt[1], inv[0]).astype(BF16)

    def row_step(j, _):
        cols = pl.ds(pl.multiple_of(j * NB, NB), NB)
        b_buf[1, :, cols] = (
            b_buf[1, :, cols].astype(F32) - dot(panel_d, b_buf[0, :, cols])
        ).astype(BF16)
        return 0

    lax.fori_loop(0, SIDE, row_step, 0)
    tab_cp.wait()

    def x_copy(q, d):
        k = OFFSETS.index(d)
        return pltpu.make_async_remote_copy(
            s_bufs[q].at[pl.ds(2 * k, 2)],
            r_bufs[q].at[pl.ds(2 * k, 2)],
            x_ss.at[q, k],
            x_rs.at[q, k],
            device_id=(peer(d), r, c),
            device_id_type=MESH,
        )

    f_cps = []
    for q in range(NQ):
        size = CHUNKS[q]

        @pl.when(c == 0)
        def _():
            c_loc[q].wait()

        for row in range(2):

            @pl.when((r == row) & (c == 1))
            def _():
                c_copy(q, 1 - row).wait_recv()

        first = c_bufs[q][:, :, pl.ds(0, NB)].reshape(SIDE * size, NB)
        second = c_bufs[q][:, :, pl.ds(NB, NB)].reshape(SIDE * size, NB)
        panel0 = dot(first, inv[0]).astype(BF16)
        second = (second.astype(F32) - dot(panel0, dt[0])).astype(BF16)
        panel1 = dot(second, inv[1])
        line = lax.broadcasted_iota(jnp.int32, panel1.shape, 0)
        panel1 = jnp.where((line < size) & (r == 0), 0.0, panel1).astype(BF16)
        l_buf[pl.ds(0, SIDE * size), pl.ds(0, NB)] = panel0
        l_buf[pl.ds(0, SIDE * size), pl.ds(NB, NB)] = panel1

        @pl.when(c == 0)
        def _():
            f_bufs[q][...] = panel0.reshape(SIDE, size, NB)

        @pl.when(c == 1)
        def _():
            f_bufs[q][...] = panel1.reshape(SIDE, size, NB)

        f_cp = pltpu.make_async_copy(f_bufs[q], fac_out.at[:, rows(q), :], f_sem.at[q])
        f_cp.start()
        f_cps.append(f_cp)
        a_cps[q].wait()

        def tile_step(j, _):
            cols = pl.ds(pl.multiple_of(j * NB, NB), NB)
            both = b_buf[:, :, cols].reshape(2 * NB, NB)
            prod = dot(l_buf[pl.ds(0, SIDE * size), :], both)
            block = a_bufs[q][:, :, cols].astype(F32).reshape(SIDE * size, NB)
            block = (block - prod).astype(BF16).reshape(SIDE, size, NB)
            for i in range(SIDE):
                tiles[i * SIDE + j, pl.ds(0, size), :] = block[i]
            return 0

        lax.fori_loop(0, SIDE, tile_step, 0)

        for s in range(2):
            r_bufs[q][s] = tiles[tab_s[0, 2 * me + s], pl.ds(0, size), :]
        for d in ORDER:
            k = OFFSETS.index(d)
            g = peer(d)
            for s in range(2):
                s_bufs[q][2 * k + s] = tiles[tab_s[0, 2 * g + s], pl.ds(0, size), :]
            x_copy(q, d).start()

    for d in ORDER:
        pos_copy(d).wait_recv()
    got = pos_recv[...]
    lane8 = lax.broadcasted_iota(jnp.int32, (GROUPS * 8, 128), 1)

    def slot_of(v):
        return jnp.where(v >= 0, (v >> 3) * 2 + (v & 1), -1)

    last = jnp.max(jnp.where(got == lane8, sub8, -1), axis=0, keepdims=True)
    got_v[pl.ds(0, 8), :] = jnp.broadcast_to(slot_of(last), (8, 128))
    eye = lax.broadcasted_iota(jnp.int32, (128, 128), 0) == lax.broadcasted_iota(
        jnp.int32, (128, 128), 1
    )
    for h in range(2):
        own = jnp.sum(
            jnp.where(eye, got[h * 128 : (h + 1) * 128], 0), axis=0, keepdims=True
        )
        prev = jnp.max(
            jnp.where((got == own) & (sub8 < lane8 + h * 128), sub8, -1), axis=0, keepdims=True
        )
        prev = jnp.where(own >= 0, prev, -1)
        got_v[pl.ds(8 + 8 * h, 8), :] = jnp.broadcast_to(slot_of(prev), (8, 128))
    got_cp = pltpu.make_async_copy(got_v, got_s, t_sem.at[1])
    got_cp.start()
    got_cp.wait()

    o_cps = []
    for q in range(NQ):
        size = CHUNKS[q]
        for d in ORDER:
            x_copy(q, d).wait_recv()

        def add_step(i, _):
            j = (i // 2) * 8 + i % 2
            prev = got_s[8 + 8 * (j // 128), j % 128]
            so_far = acc[jnp.maximum(prev, 0), pl.ds(0, size), :]
            acc[i, pl.ds(0, size), :] = r_bufs[q][i].astype(F32) + jnp.where(
                prev >= 0, so_far, 0.0
            )
            return 0

        lax.fori_loop(0, TILES, add_step, 0)
        p_cps[q].wait()

        def out_step(p, _):
            last = got_s[0, p]
            total = acc[jnp.maximum(last, 0), pl.ds(0, size), :]
            cols = pl.ds(pl.multiple_of((p % SIDE) * NB, NB), NB)
            p_bufs[q][p // SIDE, :, cols] = (
                p_bufs[q][p // SIDE, :, cols].astype(F32) + jnp.where(last >= 0, total, 0.0)
            ).astype(BF16)
            return 0

        lax.fori_loop(0, TILES, out_step, 0)
        o_cp = pltpu.make_async_copy(p_bufs[q], out.at[:, rows(q), :], o_sem.at[q])
        o_cp.start()
        o_cps.append(o_cp)

    for cp in f_cps + o_cps:
        cp.wait()
    for d in ORDER:
        pos_copy(d).wait_send()
        for q in range(NQ):
            x_copy(q, d).wait_send()

    @pl.when((r == 0) & (c == 0))
    def _():
        for row in range(2):
            for i in range(2):
                dt_copy(i, row).wait_send()

    @pl.when(r == 0)
    def _():
        b_copy.wait_send()

    for row in range(2):

        @pl.when((r == row) & (c == 0))
        def _():
            for q in range(NQ):
                c_copy(q, 1 - row).wait_send()


def body(front, inverses, routes, positions, parent):
    hbm = pl.BlockSpec(memory_space=pl.ANY)
    smem = pl.BlockSpec(memory_space=pltpu.SMEM)
    most = max(CHUNKS)
    dma = pltpu.SemaphoreType.DMA

    def per_chunk(shape):
        return [pltpu.VMEM(shape(n), BF16) for n in CHUNKS]

    scratch = (
        per_chunk(lambda n: (SIDE, n, 2 * NB))
        + per_chunk(lambda n: (SIDE, n, WIDTH))
        + per_chunk(lambda n: (SIDE, n, WIDTH))
        + per_chunk(lambda n: (SIDE, n, NB))
        + per_chunk(lambda n: (TILES, n, NB))
        + per_chunk(lambda n: (TILES, n, NB))
        + [
            pltpu.VMEM((2, NB, WIDTH), BF16),
            pltpu.VMEM((2, NB, NB), BF16),
            pltpu.VMEM((SIDE * most, 2 * NB), BF16),
            pltpu.VMEM((TILES, most, NB), BF16),
            pltpu.VMEM((TILES, most, NB), F32),
            pltpu.VMEM((GROUPS * 8, 128), jnp.int32),
            pltpu.VMEM((GROUPS * 8, 128), jnp.int32),
            pltpu.VMEM((8, 128), jnp.int32),
            pltpu.SMEM((8, 128), jnp.int32),
            pltpu.VMEM((24, 128), jnp.int32),
            pltpu.SMEM((24, 128), jnp.int32),
        ]
        + [dma((NQ,))] * 6
        + [dma((NQ, GROUPS))] * 2
        + [dma((GROUPS,))] * 2
        + [dma, dma, dma((2, 2)), dma((2,)), dma((2,))]
    )
    factor, added = pl.pallas_call(
        kernel,
        out_shape=(
            jax.ShapeDtypeStruct((SIDE, NB, NB), BF16),
            jax.ShapeDtypeStruct((SIDE, NB, WIDTH), BF16),
        ),
        in_specs=[hbm, pl.BlockSpec(memory_space=pltpu.VMEM), smem, smem, hbm],
        out_specs=(hbm, hbm),
        scratch_shapes=scratch,
        compiler_params=pltpu.CompilerParams(
            collective_id=0, has_side_effects=True, vmem_limit_bytes=60 * 2**20
        ),
        cost_estimate=pl.CostEstimate(
            flops=2 * WIDTH * WIDTH * 2 * NB, bytes_accessed=25 * 2**20, transcendentals=0
        ),
        name="eliminate_exchange_add",
    )(
        front.reshape(SIDE, NB, WIDTH),
        inverses[0],
        routes[0],
        positions[0],
        parent.reshape(SIDE, NB, WIDTH),
    )
    return factor.reshape(1, WIDTH, NB), added.reshape(1, WIDTH, WIDTH)


def solution(mesh):
    return jax.shard_map(
        body,
        mesh=mesh,
        in_specs=(
            P("front", "row", "col"),
            P("front", None, None, None),
            P("front", "row", "col"),
            P("front", "row", "col"),
            P("front", "row", "col"),
        ),
        out_specs=(P("front", "row", "col"), P("front", "row", "col")),
        check_vma=False,
    )
```

time: 612 us -> 169 us (0.28)
  waiting for transfers between devices: 409 us -> 0 us
  Pallas kernels: 0 us -> 156 us
  local copies, waits for them, and re-layouts: 94.4 us -> 10.7 us
  matrix products: 67.1 us -> 0 us
  starting transfers between devices: 17.1 us -> 0 us
  between operations: 13.9 us -> 0.64 us
  other arithmetic: 9.15 us -> 0 us
    all_to_all x2 -> x0, waiting for transfers between devices: 271 us -> none  [the longest x1 271 us: body(): lax.all_to_all(outgoing, 'front', split_axis=0, concat_axis=0, tiled=True)]
    pallas_call x0 -> x1, Pallas kernels: none -> 156 us  [body(): pl.pallas_call(kernel, out_shape=(jax.ShapeDtypeStruct((SIDE, NB, NB), BF...]
    psum x4 -> x0, waiting for transfers between devices: 138 us -> none  [from_root(): return lax.psum(kept, axis)]
    dot_general x7 -> x0, matrix products: 67.1 us -> none  [the longest x2 28.4 us: body(): jnp.dot(panel_factor, block_row, preferred_element_type=jnp.float32)]
    dot_general x1 -> x0, local copies, waits for them, and re-layouts: 28.5 us -> none  [body(): jnp.dot(send_table.T, tiles, precision=lax.Precision.HIGHEST, preferred_e...]
    unnamed x10 -> x2, local copies, waits for them, and re-layouts: 32.5 us -> 10.7 us
    reshape x1 -> x0, local copies, waits for them, and re-layouts: 17.6 us -> none  [body(): incoming.reshape(slot_count, tile_area)]
    all_to_all x2 -> x0, starting transfers between devices: 16.9 us -> none  [the longest x1 8.5 us: body(): lax.all_to_all(outgoing, 'front', split_axis=0, concat_axis=0, tiled=True)]
  transfers between devices with their start and end apart: 6 -> 0, of which waited for: 5 -> 0; matrix products, arithmetic and copies ran while one was open for 17% -> 0% of each run, Pallas kernels for 0% -> 0%
where the time goes in v1:
time: 169 us; the launch traced here: 167 us
  Pallas kernels  156 us (92%)
  local copies, waits for them, and re-layouts  10.7 us (6%)
    pallas_call x1, Pallas kernels, body(): pl.pallas_call(kernel, out_shape=(jax.ShapeDtypeStruct((SIDE, NB, NB), BF...  156 us
    unnamed x2, local copies, waits for them, and re-layouts  10.7 us

profile of v1, /device:TPU:26, one launch (start us, length us, event | category | flops | bytes accessed | tf_op | source)
XLA Modules:
  0.0 166.9 jit_solution(5664945376838021445)
XLA Ops:
  0.6 155.6 %eliminate_exchange_add.1 = (bf16[8,256,256]{2,1,0:T(8,128)(2,1)}, bf16[8,256,2048]{2,1,0:T(8,128)(2,1)}) custom-call(bf16[8,256,2048]{2,1,0:T(8,128)(2,1)} %bitcast.8, bf16[2,256,256]{2,1,0:T(8,128)(2,1)} %bitcast.11, s32[8,8]{1,0:T(8,128)} %bitcast.12, s32[8,8]{1,0:T(8,128)} %bitcast.13, bf16[8,256,2048]{2,1,0:T(8,128)(2,1)} %bitcast.9), custom_call_target="tpu_custom_call" | custom-call | flops 4294967296 | bytes 26214400 | tf_op jit(solution)/shard_map/eliminate_exchange_add/pallas_call | solution.py:408
  156.2 2.3 %copy.9 = bf16[1,2048,256]{2,1,0:T(8,128)(2,1)} copy(bf16[1,2048,256]{2,1,0:T(8,128)(2,1)} %bitcast.10) | data formatting | bytes 2097152
  158.5 8.4 %copy.10 = bf16[1,2048,2048]{2,1,0:T(8,128)(2,1)} copy(bf16[1,2048,2048]{2,1,0:T(8,128)(2,1)} %bitcast.7) | data formatting | bytes 16777216

commit v2 on v1

--- a/solution.py
+++ b/solution.py
@@ -13,7 +13,8 @@
 TILES = SIDE * SIDE
 GROUPS = 32
 WIDTH = SIDE * NB
-CHUNKS = (64, 64, 64, 64)
+CHUNKS = (16, 32, 64, 48, 48, 32, 16)
+RELAY = (4, 5, 6)
 STARTS = tuple(sum(CHUNKS[:q]) for q in range(len(CHUNKS)))
 NQ = len(CHUNKS)
 F32 = jnp.float32
@@ -25,11 +26,38 @@
 
 
 OFFSETS = [(z, y, x) for z in range(4) for y in range(4) for x in range(2)]
-ORDER = sorted(OFFSETS[1:], key=lambda d: -hops(d))
+STRAIGHT = sorted([d for d in OFFSETS[1:] if d[2] == 0], key=lambda d: -hops(d))
+ACROSS = sorted([d for d in OFFSETS if d[2] == 1], key=lambda d: -hops(d))
+ORDER = ACROSS + STRAIGHT
+HELD = min(RELAY)
 
 
 def dot(a, b):
     return jnp.dot(a, b, preferred_element_type=F32)
+
+
+def chain(got, arrived, acc, size):
+    def step(i, _):
+        j = (i // 2) * 8 + i % 2
+        prev = got[8 + 8 * (j // 128), j % 128]
+        so_far = acc[jnp.maximum(prev, 0), pl.ds(0, size), :]
+        acc[i, pl.ds(0, size), :] = arrived[i].astype(F32) + jnp.where(prev >= 0, so_far, 0.0)
+        return 0
+
+    lax.fori_loop(0, TILES, step, 0)
+
+
+def place_all(got, acc, base, size):
+    def step(p, _):
+        last = got[0, p]
+        total = acc[jnp.maximum(last, 0), pl.ds(0, size), :]
+        cols = pl.ds(pl.multiple_of((p % SIDE) * NB, NB), NB)
+        base[p // SIDE, :, cols] = (
+            base[p // SIDE, :, cols].astype(F32) + jnp.where(last >= 0, total, 0.0)
+        ).astype(BF16)
+        return 0
+
+    lax.fori_loop(0, TILES, step, 0)
 
 
 def kernel(front, inv, routes, places, parent, fac_out, out, *refs):
@@ -40,10 +68,11 @@
         del refs[:n]
         return got
 
-    c_bufs, a_bufs, p_bufs, f_bufs, s_bufs, r_bufs = (take(NQ) for _ in range(6))
+    c_bufs, a_bufs, s_bufs, r_bufs = (take(NQ) for _ in range(4))
+    by_bufs = dict(zip(RELAY, take(len(RELAY)), strict=True))
     (b_buf, dt, l_buf, tiles, acc, pos_send, pos_recv, tab_v, tab_s, got_v, got_s) = take(11)
-    (c_ss, c_rs, a_sem, p_sem, f_sem, o_sem, x_ss, x_rs, pos_ss, pos_rs) = take(10)
-    (b_ss, b_rs, dt_ss, dt_rs, t_sem) = take(5)
+    (c_ss, c_rs, a_sem, p_sem, x_ss, x_rs, pos_ss, pos_rs) = take(8)
+    (b_ss, b_rs, dt_ss, dt_rs, t_sem, by_ss, by_rs) = take(7)
 
     me = lax.axis_index("front")
     r = lax.axis_index("row")
@@ -61,7 +90,8 @@
         pltpu.make_async_copy(front.at[:, rows(q), :], a_bufs[q], a_sem.at[q]) for q in range(NQ)
     ]
     p_cps = [
-        pltpu.make_async_copy(parent.at[:, rows(q), :], p_bufs[q], p_sem.at[q]) for q in range(NQ)
+        pltpu.make_async_copy(parent.at[:, rows(q), :], out.at[:, rows(q), :], p_sem.at[q])
+        for q in range(NQ)
     ]
     c_loc = [
         pltpu.make_async_copy(front.at[:, rows(q), pl.ds(0, 2 * NB)], c_bufs[q], c_rs.at[q])
@@ -75,11 +105,9 @@
 
     @pl.when(c == 0)
     def _():
-        for cp in c_loc:
-            cp.start()
-
-    for cp in a_cps:
-        cp.start()
+        c_loc[0].start()
+
+    a_cps[0].start()
 
     bar = pltpu.get_barrier_semaphore()
 
@@ -93,55 +121,8 @@
     pl.semaphore_signal(bar, 1, device_id=(me, 1 - r, c), device_id_type=MESH)
     pl.semaphore_signal(bar, 1, device_id=(me, r, 1 - c), device_id_type=MESH)
     pl.semaphore_signal(bar, 1, device_id=(me, 1 - r, 1 - c), device_id_type=MESH)
-    pl.semaphore_wait(bar, GROUPS + 2)
-
-    def dt_copy(i, row):
-        if i == 0:
-            src = front.at[0, :, pl.ds(NB, NB)]
-        else:
-            src = front.at[1, :, pl.ds(0, NB)]
-        return pltpu.make_async_remote_copy(
-            src, dt.at[i], dt_ss.at[i, row], dt_rs.at[i], device_id=(me, row, 1), device_id_type=MESH
-        )
-
-    def c_copy(q, low):
-        return pltpu.make_async_remote_copy(
-            front.at[pl.ds(low, SIDE - low), rows(q), pl.ds(0, 2 * NB)],
-            c_bufs[q].at[pl.ds(low, SIDE - low)],
-            c_ss.at[q],
-            c_rs.at[q],
-            device_id=(me, r, 1),
-            device_id_type=MESH,
-        )
-
-    b_copy = pltpu.make_async_remote_copy(
-        front.at[pl.ds(0, 2)], b_buf, b_ss, b_rs, device_id=(me, 1, c), device_id_type=MESH
-    )
-
-    @pl.when((r == 0) & (c == 0))
-    def _():
-        for row in range(2):
-            for i in range(2):
-                dt_copy(i, row).start()
-
-    @pl.when(r == 0)
-    def _():
-        b_copy.start()
-
-    for row in range(2):
-
-        @pl.when((r == row) & (c == 0))
-        def _():
-            for q in range(NQ):
-                c_copy(q, 1 - row).start()
-
-    for cp in p_cps:
-        cp.start()
-
-    @pl.when((r == 0) & (c == 1))
-    def _():
-        for q in range(NQ):
-            c_bufs[q][0] = jnp.zeros((CHUNKS[q], 2 * NB), BF16)
+    other = me + 1 - 2 * x
+    pl.semaphore_signal(bar, 1, device_id=(other, r, 1 - c), device_id_type=MESH)
 
     lane = lax.broadcasted_iota(jnp.int32, (TILES, 128), 1)
     sub = lax.broadcasted_iota(jnp.int32, (TILES, 128), 0)
@@ -174,20 +155,96 @@
     tab_cp.start()
     pos_recv[pl.ds(0, 8), :] = pos_send[pl.ds(pl.multiple_of(me * 8, 8), 8), :]
 
+    pl.semaphore_wait(bar, GROUPS + 3)
+
+    def dt_copy(i, row):
+        if i == 0:
+            src = front.at[0, :, pl.ds(NB, NB)]
+        else:
+            src = front.at[1, :, pl.ds(0, NB)]
+        return pltpu.make_async_remote_copy(
+            src, dt.at[i], dt_ss.at[i, row], dt_rs.at[i], device_id=(me, row, 1), device_id_type=MESH
+        )
+
+    def c_copy(q, low):
+        return pltpu.make_async_remote_copy(
+            front.at[pl.ds(low, SIDE - low), rows(q), pl.ds(0, 2 * NB)],
+            (by_bufs if q in RELAY else c_bufs)[q].at[pl.ds(low, SIDE - low)],
+            c_ss.at[q],
+            (by_rs if q in RELAY else c_rs).at[q],
+            device_id=(other if q in RELAY else me, r, 1),
+            device_id_type=MESH,
+        )
+
+    def by_copy(q, low):
+        return pltpu.make_async_remote_copy(
+            by_bufs[q].at[pl.ds(low, SIDE - low)],
+            c_bufs[q].at[pl.ds(low, SIDE - low)],
+            by_ss.at[q],
+            c_rs.at[q],
+            device_id=(other, r, 1),
+            device_id_type=MESH,
+        )
+
+    def send_columns(q):
+        for row in range(2):
+
+            @pl.when((r == row) & (c == 0))
+            def _():
+                if q == 1:
+                    c_copy(0, 1 - row).wait_send()
+                if q > 2:
+                    c_copy(q - 2, 1 - row).wait_send()
+                c_copy(q, 1 - row).start()
+
+    def forward(q):
+        for row in range(2):
+
+            @pl.when((r == row) & (c == 1))
+            def _():
+                c_copy(q, 1 - row).wait_recv()
+                by_copy(q, 1 - row).start()
+
+    b_copy = pltpu.make_async_remote_copy(
+        front.at[pl.ds(0, 2)], b_buf, b_ss, b_rs, device_id=(me, 1, c), device_id_type=MESH
+    )
+
+    @pl.when((r == 0) & (c == 0))
+    def _():
+        for row in range(2):
+            for i in range(2):
+                dt_copy(i, row).start()
+
+    @pl.when(r == 0)
+    def _():
+        b_copy.start()
+
+    send_columns(0)
+
+    for q in range(1, NQ):
+
+        @pl.when(c == 0)
+        def _():
+            c_loc[q].start()
+
+        a_cps[q].start()
+
+    @pl.when((r == 0) & (c == 1))
+    def _():
+        for q in range(NQ):
+            c_bufs[q][0] = jnp.zeros((CHUNKS[q], 2 * NB), BF16)
+
     def pos_copy(d):
         k = OFFSETS.index(d)
         g = peer(d)
         return pltpu.make_async_remote_copy(
             pos_send.at[pl.ds(pl.multiple_of(g * 8, 8), 8)],
             pos_recv.at[pl.ds(8 * k, 8)],
-            pos_ss.at[k],
-            pos_rs.at[k],
+            pos_ss,
+            pos_rs,
             device_id=(g, r, c),
             device_id_type=MESH,
         )
-
-    for d in ORDER:
-        pos_copy(d).start()
 
     @pl.when(r == 0)
     def _():
@@ -217,6 +274,7 @@
         return 0
 
     lax.fori_loop(0, SIDE, row_step, 0)
+    send_columns(1)
     tab_cp.wait()
 
     def x_copy(q, d):
@@ -224,13 +282,12 @@
         return pltpu.make_async_remote_copy(
             s_bufs[q].at[pl.ds(2 * k, 2)],
             r_bufs[q].at[pl.ds(2 * k, 2)],
-            x_ss.at[q, k],
-            x_rs.at[q, k],
+            x_ss.at[q],
+            x_rs.at[q],
             device_id=(peer(d), r, c),
             device_id_type=MESH,
         )
 
-    f_cps = []
     for q in range(NQ):
         size = CHUNKS[q]
 
@@ -242,7 +299,7 @@
 
             @pl.when((r == row) & (c == 1))
             def _():
-                c_copy(q, 1 - row).wait_recv()
+                (by_copy if q in RELAY else c_copy)(q, 1 - row).wait_recv()
 
         first = c_bufs[q][:, :, pl.ds(0, NB)].reshape(SIDE * size, NB)
         second = c_bufs[q][:, :, pl.ds(NB, NB)].reshape(SIDE * size, NB)
@@ -256,15 +313,12 @@
 
         @pl.when(c == 0)
         def _():
-            f_bufs[q][...] = panel0.reshape(SIDE, size, NB)
+            fac_out[:, rows(q), :] = panel0.reshape(SIDE, size, NB)
 
         @pl.when(c == 1)
         def _():
-            f_bufs[q][...] = panel1.reshape(SIDE, size, NB)
-
-        f_cp = pltpu.make_async_copy(f_bufs[q], fac_out.at[:, rows(q), :], f_sem.at[q])
-        f_cp.start()
-        f_cps.append(f_cp)
+            fac_out[:, rows(q), :] = panel1.reshape(SIDE, size, NB)
+
         a_cps[q].wait()
 
         def tile_step(j, _):
@@ -281,15 +335,59 @@
 
         for s in range(2):
             r_bufs[q][s] = tiles[tab_s[0, 2 * me + s], pl.ds(0, size), :]
-        for d in ORDER:
+        for d in STRAIGHT + ACROSS if q < HELD else ORDER:
             k = OFFSETS.index(d)
             g = peer(d)
             for s in range(2):
                 s_bufs[q][2 * k + s] = tiles[tab_s[0, 2 * g + s], pl.ds(0, size), :]
-            x_copy(q, d).start()
-
-    for d in ORDER:
-        pos_copy(d).wait_recv()
+            if q < HELD and d in ACROSS:
+
+                @pl.when(c == 1)
+                def _():
+                    x_copy(q, d).start()
+
+            else:
+                x_copy(q, d).start()
+        if q == 0:
+            for d in ORDER:
+                pos_copy(d).start()
+            for cp in p_cps:
+                cp.start()
+        if q + 2 < NQ:
+            send_columns(q + 2)
+        if q == HELD - 1:
+            for by in RELAY:
+                forward(by)
+
+            @pl.when(c == 0)
+            def _():
+                for early in range(HELD):
+                    for d in ACROSS:
+                        x_copy(early, d).start()
+
+    def all_pos():
+        some = pl.ds(8, 8 * (GROUPS - 1))
+        return pltpu.make_async_remote_copy(
+            pos_send.at[some],
+            pos_recv.at[some],
+            pos_ss,
+            pos_rs,
+            device_id=(other, r, c),
+            device_id_type=MESH,
+        )
+
+    def all_x(q):
+        some = pl.ds(2, 2 * (GROUPS - 1))
+        return pltpu.make_async_remote_copy(
+            s_bufs[q].at[some],
+            r_bufs[q].at[some],
+            x_ss.at[q],
+            x_rs.at[q],
+            device_id=(other, r, c),
+            device_id_type=MESH,
+        )
+
+    all_pos().wait_recv()
     got = pos_recv[...]
     lane8 = lax.broadcasted_iota(jnp.int32, (GROUPS * 8, 128), 1)
 
@@ -313,46 +411,7 @@
     got_cp = pltpu.make_async_copy(got_v, got_s, t_sem.at[1])
     got_cp.start()
     got_cp.wait()
-
-    o_cps = []
-    for q in range(NQ):
-        size = CHUNKS[q]
-        for d in ORDER:
-            x_copy(q, d).wait_recv()
-
-        def add_step(i, _):
-            j = (i // 2) * 8 + i % 2
-            prev = got_s[8 + 8 * (j // 128), j % 128]
-            so_far = acc[jnp.maximum(prev, 0), pl.ds(0, size), :]
-            acc[i, pl.ds(0, size), :] = r_bufs[q][i].astype(F32) + jnp.where(
-                prev >= 0, so_far, 0.0
-            )
-            return 0
-
-        lax.fori_loop(0, TILES, add_step, 0)
-        p_cps[q].wait()
-
-        def out_step(p, _):
-            last = got_s[0, p]
-            total = acc[jnp.maximum(last, 0), pl.ds(0, size), :]
-            cols = pl.ds(pl.multiple_of((p % SIDE) * NB, NB), NB)
-            p_bufs[q][p // SIDE, :, cols] = (
-                p_bufs[q][p // SIDE, :, cols].astype(F32) + jnp.where(last >= 0, total, 0.0)
-            ).astype(BF16)
-            return 0
-
-        lax.fori_loop(0, TILES, out_step, 0)
-        o_cp = pltpu.make_async_copy(p_bufs[q], out.at[:, rows(q), :], o_sem.at[q])
-        o_cp.start()
-        o_cps.append(o_cp)
-
-    for cp in f_cps + o_cps:
-        cp.wait()
-    for d in ORDER:
-        pos_copy(d).wait_send()
-        for q in range(NQ):
-            x_copy(q, d).wait_send()
-
+    all_pos().wait_send()
     @pl.when((r == 0) & (c == 0))
     def _():
         for row in range(2):
@@ -367,26 +426,41 @@
 
         @pl.when((r == row) & (c == 0))
         def _():
-            for q in range(NQ):
+            for q in range(NQ - 2, NQ):
                 c_copy(q, 1 - row).wait_send()
+
+        @pl.when((r == row) & (c == 1))
+        def _():
+            for q in RELAY:
+                by_copy(q, 1 - row).wait_send()
+
+    for q in range(NQ):
+        if q == NQ - 1:
+            for sent in range(NQ - 1):
+                all_x(sent).wait_send()
+        all_x(q).wait_recv()
+        chain(got_s, r_bufs[q], acc, CHUNKS[q])
+        p_cps[q].wait()
+        place_all(got_s, acc, out.at[:, rows(q), :], CHUNKS[q])
+    all_x(NQ - 1).wait_send()
 
 
 def body(front, inverses, routes, positions, parent):
     hbm = pl.BlockSpec(memory_space=pl.ANY)
     smem = pl.BlockSpec(memory_space=pltpu.SMEM)
+    vmem = pl.BlockSpec(memory_space=pltpu.VMEM)
     most = max(CHUNKS)
     dma = pltpu.SemaphoreType.DMA
 
-    def per_chunk(shape):
-        return [pltpu.VMEM(shape(n), BF16) for n in CHUNKS]
+    def per_chunk(shape, chunks=CHUNKS):
+        return [pltpu.VMEM(shape(n), BF16) for n in chunks]
 
     scratch = (
         per_chunk(lambda n: (SIDE, n, 2 * NB))
         + per_chunk(lambda n: (SIDE, n, WIDTH))
-        + per_chunk(lambda n: (SIDE, n, WIDTH))
-        + per_chunk(lambda n: (SIDE, n, NB))
         + per_chunk(lambda n: (TILES, n, NB))
         + per_chunk(lambda n: (TILES, n, NB))
+        + per_chunk(lambda n: (SIDE, n, 2 * NB), [CHUNKS[q] for q in RELAY])
         + [
             pltpu.VMEM((2, NB, WIDTH), BF16),
             pltpu.VMEM((2, NB, NB), BF16),
@@ -401,21 +475,20 @@
             pltpu.SMEM((24, 128), jnp.int32),
         ]
         + [dma((NQ,))] * 6
-        + [dma((NQ, GROUPS))] * 2
-        + [dma((GROUPS,))] * 2
-        + [dma, dma, dma((2, 2)), dma((2,)), dma((2,))]
+        + [dma, dma]
+        + [dma, dma, dma((2, 2)), dma((2,)), dma((2,)), dma((NQ,)), dma((NQ,))]
     )
     factor, added = pl.pallas_call(
         kernel,
         out_shape=(
-            jax.ShapeDtypeStruct((SIDE, NB, NB), BF16),
-            jax.ShapeDtypeStruct((SIDE, NB, WIDTH), BF16),
+            pltpu.VMEM((SIDE, NB, NB), BF16),
+            pltpu.VMEM((SIDE, NB, WIDTH), BF16),
         ),
-        in_specs=[hbm, pl.BlockSpec(memory_space=pltpu.VMEM), smem, smem, hbm],
-        out_specs=(hbm, hbm),
+        in_specs=[hbm, vmem, smem, smem, hbm],
+        out_specs=(vmem, vmem),
         scratch_shapes=scratch,
         compiler_params=pltpu.CompilerParams(
-            collective_id=0, has_side_effects=True, vmem_limit_bytes=60 * 2**20
+            collective_id=0, has_side_effects=True, vmem_limit_bytes=50 * 2**20
         ),
         cost_estimate=pl.CostEstimate(
             flops=2 * WIDTH * WIDTH * 2 * NB, bytes_accessed=25 * 2**20, transcendentals=0

time: 169 us -> 143 us (0.85)
  Pallas kernels: 156 us -> 136 us
  local copies, waits for them, and re-layouts: 10.7 us -> 4.37 us
    pallas_call x1, Pallas kernels: 156 us -> 136 us  [body(): pl.pallas_call(kernel, out_shape=(pltpu.VMEM((SIDE, NB, NB), BF16), pltpu...]
    unnamed x2, local copies, waits for them, and re-layouts: 10.7 us -> 4.37 us
where the time goes in v2:
time: 143 us; the launch traced here: 141 us
  Pallas kernels  136 us (95%)
  local copies, waits for them, and re-layouts  4.37 us (3%)
    pallas_call x1, Pallas kernels, body(): pl.pallas_call(kernel, out_shape=(pltpu.VMEM((SIDE, NB, NB), BF16), pltpu...  136 us
    unnamed x2, local copies, waits for them, and re-layouts  4.37 us

profile of v2, /device:TPU:26, one launch (start us, length us, event | category | flops | bytes accessed | tf_op | source)
XLA Modules:
  0.0 141.3 jit_solution(15684822917513815203)
XLA Ops:
  0.6 136.3 %eliminate_exchange_add.1 = (bf16[8,256,256]{2,1,0:T(8,128)(2,1)S(1)}, bf16[8,256,2048]{2,1,0:T(8,128)(2,1)S(1)}) custom-call(bf16[8,256,2048]{2,1,0:T(8,128)(2,1)} %bitcast.9, bf16[2,256,256]{2,1,0:T(8,128)(2,1)} %bitcast.11, s32[8,8]{1,0:T(8,128)} %bitcast.12, s32[8,8]{1,0:T(8,128)} %bitcast.13, bf16[8,256,2048]{2,1,0:T(8,128)(2,1)} %bitcast.10), custom_call_target="tpu_custom_call" | custom-call | flops 4294967296 | bytes 26214400 | tf_op jit(solution)/shard_map/eliminate_exchange_add/pallas_call | solution.py:481
  136.9 1.0 copy.9
  137.9 3.4 %copy.10 = bf16[1,2048,2048]{2,1,0:T(8,128)(2,1)} copy(bf16[1,2048,2048]{2,1,0:T(8,128)(2,1)S(1)} %bitcast.7) | data formatting | bytes 16777216

commit v3 on v2

--- a/solution.py
+++ b/solution.py
@@ -13,10 +13,11 @@
 TILES = SIDE * SIDE
 GROUPS = 32
 WIDTH = SIDE * NB
-CHUNKS = (16, 32, 64, 48, 48, 32, 16)
-RELAY = (4, 5, 6)
+CHUNKS = (16, 48, 48, 48, 64, 32)
+RELAY = (4, 5)
 STARTS = tuple(sum(CHUNKS[:q]) for q in range(len(CHUNKS)))
 NQ = len(CHUNKS)
+LAST = CHUNKS[-1]
 F32 = jnp.float32
 BF16 = jnp.bfloat16
 
@@ -29,7 +30,7 @@
 STRAIGHT = sorted([d for d in OFFSETS[1:] if d[2] == 0], key=lambda d: -hops(d))
 ACROSS = sorted([d for d in OFFSETS if d[2] == 1], key=lambda d: -hops(d))
 ORDER = ACROSS + STRAIGHT
-HELD = min(RELAY)
+HELD = min(RELAY) - 1
 
 
 def dot(a, b):
@@ -47,12 +48,12 @@
     lax.fori_loop(0, TILES, step, 0)
 
 
-def place_all(got, acc, base, size):
+def place_all(got, acc, base, to, size):
     def step(p, _):
         last = got[0, p]
         total = acc[jnp.maximum(last, 0), pl.ds(0, size), :]
         cols = pl.ds(pl.multiple_of((p % SIDE) * NB, NB), NB)
-        base[p // SIDE, :, cols] = (
+        to[p // SIDE, :, cols] = (
             base[p // SIDE, :, cols].astype(F32) + jnp.where(last >= 0, total, 0.0)
         ).astype(BF16)
         return 0
@@ -60,7 +61,7 @@
     lax.fori_loop(0, TILES, step, 0)
 
 
-def kernel(front, inv, routes, places, parent, fac_out, out, *refs):
+def kernel(front, inv, routes, places, parent, fac_out, out, last_out, got_v, *refs):
     refs = list(refs)
 
     def take(n):
@@ -68,9 +69,10 @@
         del refs[:n]
         return got
 
-    c_bufs, a_bufs, s_bufs, r_bufs = (take(NQ) for _ in range(4))
+    c_bufs, a_bufs, s_bufs = (take(NQ) for _ in range(3))
+    r_bufs = take(NQ - 1) + [last_out]
     by_bufs = dict(zip(RELAY, take(len(RELAY)), strict=True))
-    (b_buf, dt, l_buf, tiles, acc, pos_send, pos_recv, tab_v, tab_s, got_v, got_s) = take(11)
+    (b_buf, dt, l_buf, tiles, acc, pos_send, pos_recv, tab_v, tab_s, got_s) = take(10)
     (c_ss, c_rs, a_sem, p_sem, x_ss, x_rs, pos_ss, pos_rs) = take(8)
     (b_ss, b_rs, dt_ss, dt_rs, t_sem, by_ss, by_rs) = take(7)
 
@@ -124,6 +126,79 @@
     other = me + 1 - 2 * x
     pl.semaphore_signal(bar, 1, device_id=(other, r, 1 - c), device_id_type=MESH)
 
+    pl.semaphore_wait(bar, GROUPS + 3)
+
+    def dt_copy(i):
+        if i == 0:
+            src = front.at[0, :, pl.ds(NB, NB)]
+        else:
+            src = front.at[1, :, pl.ds(0, NB)]
+        return pltpu.make_async_remote_copy(
+            src, dt.at[i], dt_ss.at[i], dt_rs.at[i], device_id=(me, 0, 1), device_id_type=MESH
+        )
+
+    def dt_pass(i):
+        return pltpu.make_async_remote_copy(
+            dt.at[i], dt.at[i], dt_ss.at[i], dt_rs.at[i], device_id=(me, 1, 1), device_id_type=MESH
+        )
+
+    def c_copy(q, low):
+        return pltpu.make_async_remote_copy(
+            front.at[pl.ds(low, SIDE - low), rows(q), pl.ds(0, 2 * NB)],
+            (by_bufs if q in RELAY else c_bufs)[q].at[pl.ds(low, SIDE - low)],
+            c_ss.at[q],
+            (by_rs if q in RELAY else c_rs).at[q],
+            device_id=(other if q in RELAY else me, r, 1),
+            device_id_type=MESH,
+        )
+
+    def by_copy(q, low):
+        return pltpu.make_async_remote_copy(
+            by_bufs[q].at[pl.ds(low, SIDE - low)],
+            c_bufs[q].at[pl.ds(low, SIDE - low)],
+            by_ss.at[q],
+            c_rs.at[q],
+            device_id=(other, r, 1),
+            device_id_type=MESH,
+        )
+
+    left = []
+
+    def send_columns(send, after):
+        for row in range(2):
+
+            @pl.when((r == row) & (c == 0))
+            def _():
+                for q in after:
+                    c_copy(q, 1 - row).wait_send()
+                for q in send:
+                    c_copy(q, 1 - row).start()
+
+        left.extend(after)
+
+    def forward(q):
+        for row in range(2):
+
+            @pl.when((r == row) & (c == 1))
+            def _():
+                c_copy(q, 1 - row).wait_recv()
+                by_copy(q, 1 - row).start()
+
+    b_copy = pltpu.make_async_remote_copy(
+        front.at[pl.ds(0, 2)], b_buf, b_ss, b_rs, device_id=(me, 1, c), device_id_type=MESH
+    )
+
+    @pl.when((r == 0) & (c == 0))
+    def _():
+        for i in range(2):
+            dt_copy(i).start()
+
+    @pl.when(r == 0)
+    def _():
+        b_copy.start()
+
+    send_columns([0], [])
+
     lane = lax.broadcasted_iota(jnp.int32, (TILES, 128), 1)
     sub = lax.broadcasted_iota(jnp.int32, (TILES, 128), 0)
     lane1 = lax.broadcasted_iota(jnp.int32, (1, 128), 1)
@@ -155,71 +230,7 @@
     tab_cp.start()
     pos_recv[pl.ds(0, 8), :] = pos_send[pl.ds(pl.multiple_of(me * 8, 8), 8), :]
 
-    pl.semaphore_wait(bar, GROUPS + 3)
-
-    def dt_copy(i, row):
-        if i == 0:
-            src = front.at[0, :, pl.ds(NB, NB)]
-        else:
-            src = front.at[1, :, pl.ds(0, NB)]
-        return pltpu.make_async_remote_copy(
-            src, dt.at[i], dt_ss.at[i, row], dt_rs.at[i], device_id=(me, row, 1), device_id_type=MESH
-        )
-
-    def c_copy(q, low):
-        return pltpu.make_async_remote_copy(
-            front.at[pl.ds(low, SIDE - low), rows(q), pl.ds(0, 2 * NB)],
-            (by_bufs if q in RELAY else c_bufs)[q].at[pl.ds(low, SIDE - low)],
-            c_ss.at[q],
-            (by_rs if q in RELAY else c_rs).at[q],
-            device_id=(other if q in RELAY else me, r, 1),
-            device_id_type=MESH,
-        )
-
-    def by_copy(q, low):
-        return pltpu.make_async_remote_copy(
-            by_bufs[q].at[pl.ds(low, SIDE - low)],
-            c_bufs[q].at[pl.ds(low, SIDE - low)],
-            by_ss.at[q],
-            c_rs.at[q],
-            device_id=(other, r, 1),
-            device_id_type=MESH,
-        )
-
-    def send_columns(q):
-        for row in range(2):
-
-            @pl.when((r == row) & (c == 0))
-            def _():
-                if q == 1:
-                    c_copy(0, 1 - row).wait_send()
-                if q > 2:
-                    c_copy(q - 2, 1 - row).wait_send()
-                c_copy(q, 1 - row).start()
-
-    def forward(q):
-        for row in range(2):
-
-            @pl.when((r == row) & (c == 1))
-            def _():
-                c_copy(q, 1 - row).wait_recv()
-                by_copy(q, 1 - row).start()
-
-    b_copy = pltpu.make_async_remote_copy(
-        front.at[pl.ds(0, 2)], b_buf, b_ss, b_rs, device_id=(me, 1, c), device_id_type=MESH
-    )
-
-    @pl.when((r == 0) & (c == 0))
-    def _():
-        for row in range(2):
-            for i in range(2):
-                dt_copy(i, row).start()
-
-    @pl.when(r == 0)
-    def _():
-        b_copy.start()
-
-    send_columns(0)
+    send_columns([1], [0])
 
     for q in range(1, NQ):
 
@@ -246,6 +257,12 @@
             device_id_type=MESH,
         )
 
+    @pl.when((r == 0) & (c == 1))
+    def _():
+        for i in range(2):
+            dt_copy(i).wait_recv()
+            dt_pass(i).start()
+
     @pl.when(r == 0)
     def _():
         b_loc.wait()
@@ -259,10 +276,10 @@
         dt[0] = b_buf[0, :, pl.ds(NB, NB)]
         dt[1] = b_buf[1, :, pl.ds(0, NB)]
 
-    @pl.when(c == 1)
+    @pl.when((r == 1) & (c == 1))
     def _():
         for i in range(2):
-            dt_copy(i, 0).wait_recv()
+            dt_pass(i).wait_recv()
 
     panel_d = dot(dt[1], inv[0]).astype(BF16)
 
@@ -274,7 +291,7 @@
         return 0
 
     lax.fori_loop(0, SIDE, row_step, 0)
-    send_columns(1)
+    send_columns([2], [1])
     tab_cp.wait()
 
     def x_copy(q, d):
@@ -335,7 +352,7 @@
 
         for s in range(2):
             r_bufs[q][s] = tiles[tab_s[0, 2 * me + s], pl.ds(0, size), :]
-        for d in STRAIGHT + ACROSS if q < HELD else ORDER:
+        for d in ORDER:
             k = OFFSETS.index(d)
             g = peer(d)
             for s in range(2):
@@ -353,12 +370,17 @@
                 pos_copy(d).start()
             for cp in p_cps:
                 cp.start()
-        if q + 2 < NQ:
-            send_columns(q + 2)
+        if q == 1:
+            send_columns([3], [])
         if q == HELD - 1:
+            send_columns([HELD + 1], range(2, HELD))
+            send_columns([HELD + 2], [HELD])
+        elif q >= HELD and q + 3 < NQ:
+            send_columns([q + 3], [q + 1])
+        if q == min(RELAY) - 1:
             for by in RELAY:
                 forward(by)
-
+        if q == HELD - 1:
             @pl.when(c == 0)
             def _():
                 for early in range(HELD):
@@ -414,9 +436,13 @@
     all_pos().wait_send()
     @pl.when((r == 0) & (c == 0))
     def _():
-        for row in range(2):
-            for i in range(2):
-                dt_copy(i, row).wait_send()
+        for i in range(2):
+            dt_copy(i).wait_send()
+
+    @pl.when((r == 0) & (c == 1))
+    def _():
+        for i in range(2):
+            dt_pass(i).wait_send()
 
     @pl.when(r == 0)
     def _():
@@ -426,8 +452,9 @@
 
         @pl.when((r == row) & (c == 0))
         def _():
-            for q in range(NQ - 2, NQ):
-                c_copy(q, 1 - row).wait_send()
+            for q in range(NQ):
+                if q not in left:
+                    c_copy(q, 1 - row).wait_send()
 
         @pl.when((r == row) & (c == 1))
         def _():
@@ -438,11 +465,34 @@
         if q == NQ - 1:
             for sent in range(NQ - 1):
                 all_x(sent).wait_send()
+            p_cps[q].wait()
         all_x(q).wait_recv()
-        chain(got_s, r_bufs[q], acc, CHUNKS[q])
-        p_cps[q].wait()
-        place_all(got_s, acc, out.at[:, rows(q), :], CHUNKS[q])
+        if q < NQ - 1:
+            chain(got_s, r_bufs[q], acc, CHUNKS[q])
+            p_cps[q].wait()
+            place_all(got_s, acc, out.at[:, rows(q), :], out.at[:, rows(q), :], CHUNKS[q])
     all_x(NQ - 1).wait_send()
+
+
+def finish(factor, part, arrived, got, fac_out, out, got_s, acc, rest, sem):
+    done = STARTS[-1]
+    got_cp = pltpu.make_async_copy(got, got_s, sem.at[0])
+    got_cp.start()
+    moves = [pltpu.make_async_copy(factor, fac_out, sem.at[1])]
+    for i in range(SIDE):
+        ready = pl.ds(0, done)
+        moves.append(
+            pltpu.make_async_copy(part.at[i, ready, :], out.at[i, ready, :], sem.at[3 + i])
+        )
+    for cp in moves:
+        cp.start()
+    got_cp.wait()
+    chain(got_s, arrived, acc, LAST)
+    place_all(got_s, acc, part.at[:, pl.ds(done, LAST), :], rest, LAST)
+    last_cp = pltpu.make_async_copy(rest, out.at[:, pl.ds(done, LAST), :], sem.at[2])
+    last_cp.start()
+    for cp in moves + [last_cp]:
+        cp.wait()
 
 
 def body(front, inverses, routes, positions, parent):
@@ -459,7 +509,7 @@
         per_chunk(lambda n: (SIDE, n, 2 * NB))
         + per_chunk(lambda n: (SIDE, n, WIDTH))
         + per_chunk(lambda n: (TILES, n, NB))
-        + per_chunk(lambda n: (TILES, n, NB))
+        + per_chunk(lambda n: (TILES, n, NB), CHUNKS[:-1])
         + per_chunk(lambda n: (SIDE, n, 2 * NB), [CHUNKS[q] for q in RELAY])
         + [
             pltpu.VMEM((2, NB, WIDTH), BF16),
@@ -471,21 +521,22 @@
             pltpu.VMEM((GROUPS * 8, 128), jnp.int32),
             pltpu.VMEM((8, 128), jnp.int32),
             pltpu.SMEM((8, 128), jnp.int32),
-            pltpu.VMEM((24, 128), jnp.int32),
             pltpu.SMEM((24, 128), jnp.int32),
         ]
         + [dma((NQ,))] * 6
         + [dma, dma]
-        + [dma, dma, dma((2, 2)), dma((2,)), dma((2,)), dma((NQ,)), dma((NQ,))]
-    )
-    factor, added = pl.pallas_call(
+        + [dma, dma, dma((2,)), dma((2,)), dma((2,)), dma((NQ,)), dma((NQ,))]
+    )
+    factor, part, arrived, got = pl.pallas_call(
         kernel,
         out_shape=(
             pltpu.VMEM((SIDE, NB, NB), BF16),
             pltpu.VMEM((SIDE, NB, WIDTH), BF16),
+            pltpu.VMEM((TILES, LAST, NB), BF16),
+            pltpu.VMEM((24, 128), jnp.int32),
         ),
         in_specs=[hbm, vmem, smem, smem, hbm],
-        out_specs=(vmem, vmem),
+        out_specs=(vmem,) * 4,
         scratch_shapes=scratch,
         compiler_params=pltpu.CompilerParams(
             collective_id=0, has_side_effects=True, vmem_limit_bytes=50 * 2**20
@@ -501,6 +552,26 @@
         positions[0],
         parent.reshape(SIDE, NB, WIDTH),
     )
+    factor, added = pl.pallas_call(
+        finish,
+        out_shape=(
+            jax.ShapeDtypeStruct((SIDE, NB, NB), BF16),
+            jax.ShapeDtypeStruct((SIDE, NB, WIDTH), BF16),
+        ),
+        in_specs=[vmem] * 4,
+        out_specs=(hbm, hbm),
+        scratch_shapes=[
+            pltpu.SMEM((24, 128), jnp.int32),
+            pltpu.VMEM((TILES, LAST, NB), F32),
+            pltpu.VMEM((SIDE, LAST, WIDTH), BF16),
+            dma((3 + SIDE,)),
+        ],
+        compiler_params=pltpu.CompilerParams(vmem_limit_bytes=30 * 2**20),
+        cost_estimate=pl.CostEstimate(
+            flops=2 * TILES * LAST * NB, bytes_accessed=10 * 2**20, transcendentals=0
+        ),
+        name="finish",
+    )(factor, part, arrived, got)
     return factor.reshape(1, WIDTH, NB), added.reshape(1, WIDTH, WIDTH)
 
 

time: 143 us -> 137 us (0.958)
  local copies, waits for them, and re-layouts: 4.37 us -> 0 us
    pallas_call x1, Pallas kernels: 136 us -> 131 us  [body(): pl.pallas_call(kernel, out_shape=(pltpu.VMEM((SIDE, NB, NB), BF16), pltpu...]
    pallas_call x0 -> x1, Pallas kernels: none -> 4.56 us  [body(): pl.pallas_call(finish, out_shape=(jax.ShapeDtypeStruct((SIDE, NB, NB), BF...]
    unnamed x2 -> x0, local copies, waits for them, and re-layouts: 4.37 us -> none
where the time goes in v3:
time: 137 us; the launch traced here: 136 us
  Pallas kernels  135 us (99%)
    pallas_call x1, Pallas kernels, body(): pl.pallas_call(kernel, out_shape=(pltpu.VMEM((SIDE, NB, NB), BF16), pltpu...  131 us
    pallas_call x1, Pallas kernels, body(): pl.pallas_call(finish, out_shape=(jax.ShapeDtypeStruct((SIDE, NB, NB), BF...  4.56 us

profile of v3, /device:TPU:26, one launch (start us, length us, event | category | flops | bytes accessed | tf_op | source)
XLA Modules:
  0.0 135.7 jit_solution(15736362330047830321)
XLA Ops:
  0.6 130.5 %eliminate_exchange_add.1 = (bf16[8,256,256]{2,1,0:T(8,128)(2,1)S(1)}, bf16[8,256,2048]{2,1,0:T(8,128)(2,1)S(1)}, bf16[64,32,256]{2,1,0:T(8,128)(2,1)S(1)}, s32[24,128]{1,0:T(8,128)S(1)}) custom-call(bf16[8,256,2048]{2,1,0:T(8,128)(2,1)} %bitcast.7, bf16[2,256,256]{2,1,0:T(8,128)(2,1)} %bitcast.9, s32[8,8]{1,0:T(8,128)} %bitcast.10, s32[8,8]{1,0:T(8,128)} %bitcast.11, ...), custom_call_target="tpu_custom_call" | custom-call | flops 4294967296 | bytes 26214400 | tf_op jit(solution)/shard_map/eliminate_exchange_add/pallas_call | solution.py:530
  131.1 4.6 %finish.1 = (bf16[8,256,256]{2,1,0:T(8,128)(2,1)}, bf16[8,256,2048]{2,1,0:T(8,128)(2,1)}) custom-call(bf16[8,256,256]{2,1,0:T(8,128)(2,1)S(1)} %get-tuple-element.8.factor, bf16[8,256,2048]{2,1,0:T(8,128)(2,1)S(1)} %get-tuple-element.9.part, bf16[64,32,256]{2,1,0:T(8,128)(2,1)S(1)} %get-tuple-element.10.arrived, s32[24,128]{1,0:T(8,128)S(1)} %get-tuple-element.11.got), custom_call_target="tpu_custom_call" | custom-call | flops 1048576 | bytes 10485760 | tf_op jit(solution)/shard_map/finish/pallas_call | solution.py:555

commit v4 on v3

--- a/solution.py
+++ b/solution.py
@@ -45,7 +45,7 @@
         acc[i, pl.ds(0, size), :] = arrived[i].astype(F32) + jnp.where(prev >= 0, so_far, 0.0)
         return 0
 
-    lax.fori_loop(0, TILES, step, 0)
+    lax.fori_loop(0, TILES, step, 0, unroll=4)
 
 
 def place_all(got, acc, base, to, size):
@@ -58,7 +58,7 @@
         ).astype(BF16)
         return 0
 
-    lax.fori_loop(0, TILES, step, 0)
+    lax.fori_loop(0, TILES, step, 0, unroll=4)
 
 
 def kernel(front, inv, routes, places, parent, fac_out, out, last_out, got_v, *refs):

time: 137 us -> 136 us (level)
  no operation moved by 1% of the time
where the time goes in v4:
time: 136 us; the launch traced here: 135 us
  Pallas kernels  134 us (99%)
    pallas_call x1, Pallas kernels, body(): pl.pallas_call(kernel, out_shape=(pltpu.VMEM((SIDE, NB, NB), BF16), pltpu...  131 us
    pallas_call x1, Pallas kernels, body(): pl.pallas_call(finish, out_shape=(jax.ShapeDtypeStruct((SIDE, NB, NB), BF...  3.73 us

profile of v4, /device:TPU:26, one launch (start us, length us, event | category | flops | bytes accessed | tf_op | source)
XLA Modules:
  0.0 134.9 jit_solution(15208666337633952996)
XLA Ops:
  0.6 130.5 %eliminate_exchange_add.1 = (bf16[8,256,256]{2,1,0:T(8,128)(2,1)S(1)}, bf16[8,256,2048]{2,1,0:T(8,128)(2,1)S(1)}, bf16[64,32,256]{2,1,0:T(8,128)(2,1)S(1)}, s32[24,128]{1,0:T(8,128)S(1)}) custom-call(bf16[8,256,2048]{2,1,0:T(8,128)(2,1)} %bitcast.7, bf16[2,256,256]{2,1,0:T(8,128)(2,1)} %bitcast.9, s32[8,8]{1,0:T(8,128)} %bitcast.10, s32[8,8]{1,0:T(8,128)} %bitcast.11, ...), custom_call_target="tpu_custom_call" | custom-call | flops 4294967296 | bytes 26214400 | tf_op jit(solution)/shard_map/eliminate_exchange_add/pallas_call | solution.py:530
  131.1 3.7 %finish.1 = (bf16[8,256,256]{2,1,0:T(8,128)(2,1)}, bf16[8,256,2048]{2,1,0:T(8,128)(2,1)}) custom-call(bf16[8,256,256]{2,1,0:T(8,128)(2,1)S(1)} %get-tuple-element.8.factor, bf16[8,256,2048]{2,1,0:T(8,128)(2,1)S(1)} %get-tuple-element.9.part, bf16[64,32,256]{2,1,0:T(8,128)(2,1)S(1)} %get-tuple-element.10.arrived, s32[24,128]{1,0:T(8,128)S(1)} %get-tuple-element.11.got), custom_call_target="tpu_custom_call" | custom-call | flops 1048576 | bytes 10485760 | tf_op jit(solution)/shard_map/finish/pallas_call | solution.py:555
